TPU v7x, 32 devices: a whole 2x2x4 slice. The times are simulated.
32 devices in a mesh: wide: 16 (over z, x, core), narrow: 2 (over y).
Axes of the slice: x: 2, y: 2, z: 4, core: 2. Of those that a mesh axis runs over, the one named last changes fastest.
Arguments:
- spectra: bfloat16 [96, 2, 2, 4096], P('wide', None, None, 'narrow'), may hold values from -6 to 6
- dead_mask: int32 [96], P('wide'), may hold values 0 or 1
- seg_offsets: int32 [96, 2], P('wide'), may hold values from 0 to 32767
- src_index: int32 [64], replicated, may hold values from 0 to 95, as said below
Outputs:
- correlations: float32 [64, 96, 512], P('narrow', 'wide')
Inputs may be any that keep to these rules, and one draw needn't show every extreme that they name: `src_index`: source j is one of the 6 channels j // 4 * 6 to j // 4 * 6 + 5; the 4 sources of one block are distinct; source 0 is channel 0 and source 64 - 4 is channel 96 - 1.
All inputs are finite; a program needn't handle non-finite values. No bound on the sum of `dead_mask` on one device may be relied on, other than what follows from the above.
Results may differ from a plain program's by a relative error of at most 0.0013.
Values may be sent and summed in bfloat16 or wider, within the bound.
A program may use at most 128 MiB of HBM per device.

v0:
```python
import math

import jax
import jax.numpy as jnp
from jax import lax
from jax.sharding import PartitionSpec as P

NSAMP = 32768
LAGS = 512
SMOOTH = 64


EPSILON = 1e-06


def padded_2(cells, sides, width):
    for axis, dim in sides:
        count = lax.axis_size(axis)
        ends = count - 1
        head = lax.slice_in_dim(cells, 0, width, axis=dim)
        tail = lax.slice_in_dim(cells, cells.shape[dim] - width, cells.shape[dim], axis=dim)
        cells = jnp.concatenate(
            [
                lax.ppermute(tail, axis, [(i, (i + 1) % count) for i in range(ends)]),
                cells,
                lax.ppermute(head, axis, [((i + 1) % count, i) for i in range(ends)]),
            ],
            axis=dim,
        )
    return cells


def lag_table(first, length, lag_count):
    bins = first + jnp.arange(length, dtype=jnp.int32) + 1
    lag_steps = jnp.arange(lag_count, dtype=jnp.int32) - lag_count // 2 + NSAMP
    residue = bins[:, None] * lag_steps[None, :] % NSAMP
    angles = 2.0 * math.pi / NSAMP * residue.astype(jnp.float32)
    return jnp.concatenate([jnp.cos(angles), -jnp.sin(angles)], axis=0).astype(jnp.bfloat16)


def apply_whitening(real_part, imag_part, windowed, freq_bins, total_bins, dead_mask, seg_offsets):
    counts = (
        jnp.minimum(freq_bins + SMOOTH, total_bins - 1) - jnp.maximum(freq_bins - SMOOTH, 0) + 1
    ).astype(jnp.float32)
    smoothed = windowed / counts + EPSILON
    residue = (freq_bins + 1)[None, None, :] * seg_offsets[:, :, None] % NSAMP
    phase = 2.0 * math.pi / NSAMP * residue.astype(jnp.float32)
    scale = dead_mask.astype(jnp.float32)[:, None, None] / smoothed
    cosine = jnp.cos(phase)
    sine = jnp.sin(phase)
    white_real = (real_part * cosine - imag_part * sine) * scale
    white_imag = (real_part * sine + imag_part * cosine) * scale
    return jnp.stack([white_real, white_imag], axis=2).astype(jnp.bfloat16)


def cross_spectra(channels, sources, seg_count):
    chan_real = channels[:, :, 0]
    chan_imag = channels[:, :, 1]
    src_real = sources[:, :, 0]
    src_imag = sources[:, :, 1]
    cross_real = jnp.einsum(
        "ckf,skf->scf", chan_real, src_real, preferred_element_type=jnp.float32
    ) + jnp.einsum("ckf,skf->scf", chan_imag, src_imag, preferred_element_type=jnp.float32)
    cross_imag = jnp.einsum(
        "ckf,skf->scf", chan_imag, src_real, preferred_element_type=jnp.float32
    ) - jnp.einsum("ckf,skf->scf", chan_real, src_imag, preferred_element_type=jnp.float32)
    joined = jnp.concatenate([cross_real, cross_imag], axis=-1) * (1.0 / math.sqrt(seg_count))
    return joined.astype(jnp.bfloat16)


def body(spectra, dead_mask, seg_offsets, src_index):
    ch_count = spectra.shape[0]
    seg_count = spectra.shape[1]
    slice_bins = spectra.shape[3]
    narrow_count = lax.axis_size("narrow")
    wide_count = lax.axis_size("wide")
    total_bins = slice_bins * narrow_count
    narrow_pos = lax.axis_index("narrow")
    wide_pos = lax.axis_index("wide")
    freq_bins = narrow_pos * slice_bins + jnp.arange(slice_bins, dtype=jnp.int32)
    real_part = spectra[:, :, 0].astype(jnp.float32)
    imag_part = spectra[:, :, 1].astype(jnp.float32)
    amplitude = jnp.sqrt(real_part * real_part + imag_part * imag_part)
    padded = padded_2(amplitude, (("narrow", 2),), SMOOTH)
    windowed = lax.reduce_window(
        padded, jnp.zeros((), padded.dtype), lax.add, (1, 1, 2 * SMOOTH + 1), (1, 1, 1), "VALID"
    )
    whitened = apply_whitening(
        real_part, imag_part, windowed, freq_bins, total_bins, dead_mask, seg_offsets
    )
    per_block = src_index.shape[0] // wide_count
    own_rows = (
        lax.dynamic_slice_in_dim(src_index, wide_pos * per_block, per_block) - wide_pos * ch_count
    )
    selector = (own_rows[:, None] == jnp.arange(ch_count, dtype=jnp.int32)[None, :]).astype(
        jnp.bfloat16
    )
    chosen = jnp.einsum(
        "rc,ckqf->rkqf", selector, whitened, preferred_element_type=jnp.float32
    ).astype(jnp.bfloat16)
    share_rows = src_index.shape[0] // narrow_count
    norm_factor = 1.0 / math.sqrt(total_bins)
    panel = lax.all_gather(chosen, "wide", axis=0, tiled=True)
    table_part = lag_table(narrow_pos * slice_bins, slice_bins, LAGS)
    block = lax.slice_in_dim(panel, 0, share_rows * lax.axis_size("narrow"), axis=0)
    spectra_x = cross_spectra(whitened, block, seg_count)
    flat = spectra_x.reshape(share_rows * lax.axis_size("narrow") * ch_count, 2 * slice_bins)
    product = jnp.dot(flat, table_part, preferred_element_type=jnp.float32) * norm_factor
    return lax.psum_scatter(
        product.reshape(share_rows * lax.axis_size("narrow"), ch_count, LAGS),
        "narrow",
        scatter_dimension=0,
        tiled=True,
    )


def solution(mesh):
    placed = (P("wide", None, None, "narrow"), P("wide"), P("wide", None), P())
    return jax.shard_map(
        body, mesh=mesh, in_specs=placed, out_specs=P("narrow", "wide", None), check_vma=False
    )
```

profile of v0, /device:TPU:5, one launch (start us, length us, event | category | flops | bytes accessed | tf_op | source)
XLA Modules:
  0.0 723.1 jit_solution(14947062667767888711)
XLA Ops:
  6.5 1.1 fusion.50
  7.9 1.3 collective-permute-start
  9.2 4.0 collective-permute-start.1
  14.9 568.3 %reduce_window.10 = f32[6,2,1,2048]{3,2,1,0:T(1,128)S(1)} reduce-window(f32[6,2,1,2176]{3,2,1,0:T(1,128)S(1)} %copy.35, f32[]{:T(128)} %constant.57.clone.1), window={size=1x1x1x129}, to_apply=%region_0.0 | reduce-window | flops 3145728 | bytes 202756 | tf_op jit(solution)/shard_map/reduce_window | solution.py:85
  583.2 1.4 fusion.23
  585.6 19.2 %cosine_convert_fusion = (bf16[2048,512]{1,0:T(8,128)(2,1)}, bf16[2048,512]{1,0:T(8,128)(2,1)}) fusion(s32[512]{0:T(512)S(1)} %iota_add_fusion.1, s32[2048]{0:T(1024)S(1)} %get-tuple-element.16), kind=kLoop, calls=%fused_computation.17 | loop fusion | flops 17825792 | bytes 4204544 | tf_op jit(solution)/shard_map/convert
  604.8 0.9 copy.39
  605.7 0.9 copy.41
  606.6 19.9 %all-gather.2.cloned.1.call-done = bf16[64,2,2,2048]{3,2,1,0:T(2,128)(2,1)} async-done(((bf16[4,2,2,2048]{3,2,1,0:T(2,128)(2,1)}), bf16[64,2,2,2048]{3,2,1,0:T(2,128)(2,1)}) %all-gather.2.cloned.1.call-update) | async-done | bytes 1048592 | tf_op jit(solution)/shard_map/all_gather | solution.py:103
  626.6 5.4 fusion.48
  632.0 4.6 copy.50
  636.6 4.8 copy.51
  641.4 2.6 fusion.14
  644.0 4.8 fusion.12
  648.8 4.8 add_bitcast_fusion
  653.6 7.6 %copy.42 = f32[64,6,2048]{2,1,0:T(8,128)} copy(f32[64,6,2048]{0,1,2:T(8,128)} %add_bitcast_fusion) | data formatting | bytes 6291456 | tf_op jit(solution)/shard_map/add | solution.py:61
  661.2 4.8 concatenate.16
  666.1 9.2 %subtract_bitcast_fusion = f32[64,6,2048]{0,1,2:T(8,128)} fusion(f32[2048,64,6]{1,2,0:T(8,128)} %fusion.12, bf16[6,2,2048]{0,1,2:T(2,128)(2,1)S(1)} %copy.39, bf16[64,2,1,2048]{0,1,3,2:T(2,128)(2,1)S(1)} %copy-done.1), kind=kOutput, calls=%fused_computation | convolution fusion | flops 3932160 | bytes 6864896 | tf_op jit(solution)/shard_map/ckf,skf->scf/dot_general | solution.py:66
  675.3 7.7 %copy.45 = f32[64,6,2048]{2,1,0:T(8,128)} copy(f32[64,6,2048]{0,1,2:T(8,128)} %subtract_bitcast_fusion) | data formatting | bytes 6291456 | tf_op jit(solution)/shard_map/sub | solution.py:64
  683.0 5.0 concatenate.17
  688.0 5.9 fusion.16
  693.8 2.2 reshape.101
  696.1 18.0 %reduce-scatter.2.cloned.1.call-done = f32[32,6,512]{2,1,0:T(8,128)} async-done(((f32[64,6,512]{2,1,0:T(8,128)}), f32[32,6,512]{2,1,0:T(8,128)}) %reduce-scatter.2.cloned.1.call-update) | async-done | bytes 393232 | tf_op jit(solution)/shard_map/reduce_scatter | solution.py:109
  714.0 2.0 copy.46
  (22 shorter events, 2.9 us)
Async XLA Ops:
  6.5 620.0 %all-gather.2.cloned.1.call-start = ((), (), s32[]{:S(2)}) async-start(), calls=%async_computation.1 | async-start | bytes 1114112 | tf_op jit(solution)/shard_map/all_gather | solution.py:103
  7.9 6.7 collective-permute-start
  9.2 5.4 collective-permute-start.1
  585.5 128.5 %reduce-scatter.2.cloned.1.call-start = ((), (), s32[]{:S(2)}) async-start(), calls=%async_computation.2 | async-start | bytes 1572864 | tf_op jit(solution)/shard_map/reduce_scatter | solution.py:109
  644.0 4.8 copy-start
  661.2 4.8 copy-start.1
  683.0 5.0 copy-start.2
Sparse Core Ops, SparseCore 0:
  585.7 40.8 all-gather.1
  696.2 17.7 reduce-scatter.1
where the time goes:
time: 728 us; the launch traced here: 723 us
  other arithmetic  590 us (81%)
  local copies, waits for them, and re-layouts  48.1 us (7%)
  waiting for transfers between devices  37.9 us (5%)
  matrix products  27.5 us (4%)
  between operations  13.8 us (2%)
    another operation x1, other arithmetic, body(): lax.reduce_window(padded, jnp.zeros((), padded.dtype), lax.add, (1, 1, 2...  568 us
    all_gather x1, waiting for transfers between devices, body(): panel = lax.all_gather(chosen, 'wide', axis=0, tiled=True)  19.9 us
    another operation x1, other arithmetic  19.2 us
    reduce_scatter x1, waiting for transfers between devices, body(): lax.psum_scatter(product.reshape(share_rows * lax.axis_size('narrow'), ch...  18 us
  transfers between devices with their start and end apart: 4, of which 2 were waited for; matrix products, arithmetic and copies ran while one was open for 3% of the time, Pallas kernels for 0%

commit v1 on v0

--- a/solution.py
+++ b/solution.py
@@ -30,12 +30,35 @@
     return cells
 
 
+def window_sums(padded, bins):
+    step = 2 * SMOOTH
+    blocks = bins // step
+    head = padded[..., :bins].reshape(padded.shape[:-1] + (blocks, step))
+    tail = padded[..., step:].reshape(padded.shape[:-1] + (blocks, step))
+    cells = jnp.concatenate([head, tail], axis=-1)
+    ahead = jnp.arange(2 * step)[:, None] - jnp.arange(step)[None, :]
+    band = ((ahead >= 0) & (ahead <= step)).astype(jnp.float32)
+    sums = jnp.einsum("ckbi,io->ckbo", cells, band, precision=lax.Precision.HIGHEST)
+    return sums.reshape(padded.shape[:-1] + (bins,))
+
+
+def turns(product):
+    angles = 2.0 * math.pi / NSAMP * (product % NSAMP).astype(jnp.float32)
+    return jnp.cos(angles), jnp.sin(angles)
+
+
 def lag_table(first, length, lag_count):
-    bins = first + jnp.arange(length, dtype=jnp.int32) + 1
+    step = 128
     lag_steps = jnp.arange(lag_count, dtype=jnp.int32) - lag_count // 2 + NSAMP
-    residue = bins[:, None] * lag_steps[None, :] % NSAMP
-    angles = 2.0 * math.pi / NSAMP * residue.astype(jnp.float32)
-    return jnp.concatenate([jnp.cos(angles), -jnp.sin(angles)], axis=0).astype(jnp.bfloat16)
+    coarse = first + step * jnp.arange(length // step, dtype=jnp.int32)
+    fine = jnp.arange(step, dtype=jnp.int32) + 1
+    ca, sa = turns(coarse[:, None] * lag_steps[None, :])
+    cb, sb = turns(fine[:, None] * lag_steps[None, :])
+    cosine = ca[:, None] * cb[None] - sa[:, None] * sb[None]
+    sine = sa[:, None] * cb[None] + ca[:, None] * sb[None]
+    return jnp.concatenate(
+        [cosine.reshape(length, lag_count), -sine.reshape(length, lag_count)], axis=0
+    ).astype(jnp.bfloat16)
 
 
 def apply_whitening(real_part, imag_part, windowed, freq_bins, total_bins, dead_mask, seg_offsets):
@@ -82,9 +105,7 @@
     imag_part = spectra[:, :, 1].astype(jnp.float32)
     amplitude = jnp.sqrt(real_part * real_part + imag_part * imag_part)
     padded = padded_2(amplitude, (("narrow", 2),), SMOOTH)
-    windowed = lax.reduce_window(
-        padded, jnp.zeros((), padded.dtype), lax.add, (1, 1, 2 * SMOOTH + 1), (1, 1, 1), "VALID"
-    )
+    windowed = window_sums(padded, slice_bins)
     whitened = apply_whitening(
         real_part, imag_part, windowed, freq_bins, total_bins, dead_mask, seg_offsets
     )

time: 728 us -> 158 us (0.22)
  the two profiles are of different devices: /device:TPU:5 before, /device:TPU:0 now
where the time goes in v1:
time: 158 us; the launch traced here: 157 us
  waiting for transfers between devices  53.9 us (34%)
  local copies, waits for them, and re-layouts  48.1 us (30%)
  matrix products  27.8 us (18%)
  between operations  13.6 us (9%)
  other arithmetic  7.88 us (5%)
  starting transfers between devices  6.2 us (4%)
    all_gather x1, waiting for transfers between devices, body(): panel = lax.all_gather(chosen, 'wide', axis=0, tiled=True)  31.6 us
    reduce_scatter x1, waiting for transfers between devices, body(): lax.psum_scatter(product.reshape(share_rows * lax.axis_size('narrow'), ch...  19.4 us
    concatenate x2, local copies, waits for them, and re-layouts, cross_spectra(): jnp.concatenate([cross_real, cross_imag], axis=-1)  9.81 us
    unnamed x8, local copies, waits for them, and re-layouts  9.39 us
    dot_general x1, matrix products, cross_spectra(): jnp.einsum('ckf,skf->scf', chan_real, src_imag, preferred_element_type=jn...  9.22 us
    add x1, local copies, waits for them, and re-layouts, cross_spectra(): jnp.einsum('ckf,skf->scf', chan_real, src_real, preferred_element_type=jn...  7.72 us
    sub x1, local copies, waits for them, and re-layouts, cross_spectra(): jnp.einsum('ckf,skf->scf', chan_imag, src_real, preferred_element_type=jn...  7.7 us
    dot_general x1, matrix products, body(): jnp.dot(flat, table_part, preferred_element_type=jnp.float32) * norm_factor  5.86 us
  transfers between devices with their start and end apart: 4, of which 3 were waited for; matrix products, arithmetic and copies ran while one was open for 5% of the time, Pallas kernels for 0%

profile of v1, /device:TPU:0, one launch (start us, length us, event | category | flops | bytes accessed | tf_op | source)
XLA Modules:
  0.0 157.4 jit_solution(7923085989186272768)
XLA Ops:
  6.5 1.1 fusion.69
  7.9 4.9 %collective-permute-start = (f32[6,2,64]{2,0,1:T(8,128)S(1)}, f32[6,2,64]{2,0,1:T(8,128)S(1)}, u32[]{:S(2)}, u32[]{:S(2)}) collective-permute-start(f32[6,2,64]{2,0,1:T(8,128)S(1)} %get-tuple-element.13), channel_id=1, source_target_pairs={{0,1},{2,3},{4,5},{6,7},{8,9},{10,11},{12,13},{14,15},{16,17},{18,... | collective-permute-start | bytes 9224 | tf_op jit(solution)/shard_map/ppermute | solution.py:24
  12.8 1.3 collective-permute-start.1
  15.5 2.8 %collective-permute-done.1 = f32[6,2,64]{2,0,1:T(8,128)S(1)} collective-permute-done((f32[6,2,64]{2,0,1:T(8,128)S(1)}, f32[6,2,64]{2,0,1:T(8,128)S(1)}, u32[]{:S(2)}, u32[]{:S(2)}) %collective-permute-start.1) | collective-permute-done | bytes 3104 | tf_op jit(solution)/shard_map/ppermute | solution.py:26
  18.8 1.4 fusion.25
  21.5 1.1 fusion.41
  22.6 3.5 %subtract_convert_fusion = (bf16[16,128,512]{2,1,0:T(8,128)(2,1)}, bf16[16,128,512]{2,1,0:T(8,128)(2,1)}) fusion(f32[128,512]{1,0:T(8,128)S(1)} %get-tuple-element.20, f32[16,512]{1,0:T(8,128)S(1)} %get-tuple-element.18, f32[128,512]{1,0:T(8,128)S(1)} %get-tuple-element.19, f32[16,512]{1,0:T(8,128)S(1)} %get-tuple-element.17), kind=kLoop, calls=%fused_computation.9 | loop fusion | flops 9437184 | bytes 4784128 | tf_op jit(solution)/shard_map/convert.3
  27.0 0.9 copy.44
  28.0 31.6 %all-gather.2.cloned.1.call-done = bf16[64,2,2,2048]{3,2,1,0:T(2,128)(2,1)} async-done(((bf16[4,2,2,2048]{3,2,1,0:T(2,128)(2,1)}), bf16[64,2,2,2048]{3,2,1,0:T(2,128)(2,1)}) %all-gather.2.cloned.1.call-update) | async-done | bytes 1048592 | tf_op jit(solution)/shard_map/all_gather | solution.py:124
  59.6 5.4 %fusion.67 = (bf16[64,2,1,2048]{3,2,1,0:T(2,128)(2,1)}, bf16[64,2,1,2048]{3,2,1,0:T(2,128)(2,1)}) fusion(bf16[64,2,2,2048]{3,2,1,0:T(2,128)(2,1)} %all-gather.2.cloned.1.call-done), kind=kLoop, calls=%fused_computation.98 | loop fusion | bytes 2097152 | tf_op jit(solution)/shard_map/slice | solution.py:83
  65.0 4.6 %copy.57 = bf16[64,2,1,2048]{0,1,3,2:T(2,128)(2,1)S(1)} copy(bf16[64,2,1,2048]{3,2,1,0:T(2,128)(2,1)} %get-tuple-element.6) | data formatting | bytes 1048576
  69.6 4.8 %copy.58 = bf16[64,2,1,2048]{0,1,3,2:T(2,128)(2,1)} copy(bf16[64,2,1,2048]{3,2,1,0:T(2,128)(2,1)} %get-tuple-element.5) | data formatting | bytes 1048576
  74.3 2.6 %fusion.11 = f32[2048,64,6]{1,2,0:T(8,128)S(1)} fusion(bf16[6,2,2048]{0,1,2:T(2,128)(2,1)S(1)} %copy.42, bf16[64,2,1,2048]{0,1,3,2:T(2,128)(2,1)S(1)} %copy.57), kind=kOutput, calls=%fused_computation.16 | convolution fusion | flops 3145728 | bytes 3719168 | tf_op jit(solution)/shard_map/ckf,skf->scf/dot_general | solution.py:84
  77.0 4.8 %fusion.9 = f32[2048,64,6]{1,2,0:T(8,128)} fusion(bf16[6,2,2048]{0,1,2:T(2,128)(2,1)S(1)} %copy.44, bf16[64,2,1,2048]{0,1,3,2:T(2,128)(2,1)S(1)} %copy.57), kind=kOutput, calls=%fused_computation.14 | convolution fusion | flops 3145728 | bytes 3719168 | tf_op jit(solution)/shard_map/ckf,skf->scf/dot_general | solution.py:87
  81.8 4.8 %add_bitcast_fusion = f32[64,6,2048]{0,1,2:T(8,128)} fusion(f32[2048,64,6]{1,2,0:T(8,128)S(1)} %fusion.11, bf16[6,2,2048]{0,1,2:T(2,128)(2,1)S(1)} %copy.44, bf16[64,2,1,2048]{0,1,3,2:T(2,128)(2,1)S(1)} %copy-done), kind=kOutput, calls=%fused_computation.1 | convolution fusion | flops 3932160 | bytes 6864896 | tf_op jit(solution)/shard_map/ckf,skf->scf/dot_general | solution.py:86
  86.6 7.7 %copy.45 = f32[64,6,2048]{2,1,0:T(8,128)} copy(f32[64,6,2048]{0,1,2:T(8,128)} %add_bitcast_fusion) | data formatting | bytes 6291456 | tf_op jit(solution)/shard_map/add | solution.py:84
  94.3 4.8 %concatenate.25 = f32[384,2048]{1,0:T(8,128)} reshape(f32[64,6,2048]{2,1,0:T(8,128)} %copy.45) | data formatting | bytes 6291456 | tf_op jit(solution)/shard_map/concatenate | solution.py:90
  99.2 9.2 %subtract_bitcast_fusion = f32[64,6,2048]{0,1,2:T(8,128)} fusion(f32[2048,64,6]{1,2,0:T(8,128)} %fusion.9, bf16[6,2,2048]{0,1,2:T(2,128)(2,1)S(1)} %copy.42, bf16[64,2,1,2048]{0,1,3,2:T(2,128)(2,1)S(1)} %copy-done.1), kind=kOutput, calls=%fused_computation | convolution fusion | flops 3932160 | bytes 6864896 | tf_op jit(solution)/shard_map/ckf,skf->scf/dot_general | solution.py:89
  108.4 7.7 %copy.48 = f32[64,6,2048]{2,1,0:T(8,128)} copy(f32[64,6,2048]{0,1,2:T(8,128)} %subtract_bitcast_fusion) | data formatting | bytes 6291456 | tf_op jit(solution)/shard_map/sub | solution.py:87
  116.1 5.0 %concatenate.26 = f32[384,2048]{1,0:T(8,128)} reshape(f32[64,6,2048]{2,1,0:T(8,128)} %copy.48) | data formatting | bytes 6291456 | tf_op jit(solution)/shard_map/concatenate | solution.py:90
  121.1 5.9 %fusion.13 = f32[384,512]{1,0:T(8,128)} fusion(bf16[2048,512]{1,0:T(8,128)(2,1)} %bitcast.41, bf16[2048,512]{1,0:T(8,128)(2,1)} %bitcast.40, f32[384,2048]{1,0:T(8,128)} %concatenate.26, f32[384,2048]{1,0:T(8,128)S(1)} %copy-done.2), kind=kOutput, calls=%fused_computation.18 | convolution fusion | flops 1623916544 | bytes 11272192 | tf_op jit(solution)/shard_map/dot_general | solution.py:129
  126.9 2.2 %reshape.266 = f32[64,6,512]{2,1,0:T(8,128)} reshape(f32[384,512]{1,0:T(8,128)} %fusion.13) | data formatting | bytes 1572864 | tf_op jit(solution)/shard_map/reshape | solution.py:131
  129.2 19.4 %reduce-scatter.2.cloned.1.call-done = f32[32,6,512]{2,1,0:T(8,128)} async-done(((f32[64,6,512]{2,1,0:T(8,128)}), f32[32,6,512]{2,1,0:T(8,128)}) %reduce-scatter.2.cloned.1.call-update) | async-done | bytes 393232 | tf_op jit(solution)/shard_map/reduce_scatter | solution.py:130
  148.6 2.0 %copy.49 = f32[32,6,512]{2,0,1:T(8,128)} copy(f32[32,6,512]{2,1,0:T(8,128)} %reduce-scatter.2.cloned.1.call-done) | data formatting | bytes 786432 | tf_op jit(solution)/shard_map/reduce_scatter | solution.py:130
  (28 shorter events, 4.2 us)
Async XLA Ops:
  6.5 53.1 %all-gather.2.cloned.1.call-start = ((), (), s32[]{:S(2)}) async-start(), calls=%async_computation.1 | async-start | bytes 1114112 | tf_op jit(solution)/shard_map/all_gather | solution.py:124
  7.9 7.6 %collective-permute-start = (f32[6,2,64]{2,0,1:T(8,128)S(1)}, f32[6,2,64]{2,0,1:T(8,128)S(1)}, u32[]{:S(2)}, u32[]{:S(2)}) collective-permute-start(f32[6,2,64]{2,0,1:T(8,128)S(1)} %get-tuple-element.13), channel_id=1, source_target_pairs={{0,1},{2,3},{4,5},{6,7},{8,9},{10,11},{12,13},{14,15},{16,17},{18,... | collective-permute-start | bytes 9224 | tf_op jit(solution)/shard_map/ppermute | solution.py:24
  12.8 5.5 %collective-permute-start.1 = (f32[6,2,64]{2,0,1:T(8,128)S(1)}, f32[6,2,64]{2,0,1:T(8,128)S(1)}, u32[]{:S(2)}, u32[]{:S(2)}) collective-permute-start(f32[6,2,64]{2,0,1:T(8,128)S(1)} %get-tuple-element.14), channel_id=1, source_target_pairs={{1,0},{3,2},{5,4},{7,6},{9,8},{11,10},{13,12},{15,14},{17,16},{19,... | collective-permute-start | bytes 9224 | tf_op jit(solution)/shard_map/ppermute | solution.py:26
  21.2 127.4 %reduce-scatter.2.cloned.1.call-start = ((), (), s32[]{:S(2)}) async-start(), calls=%async_computation.2 | async-start | bytes 1572864 | tf_op jit(solution)/shard_map/reduce_scatter | solution.py:130
  77.0 4.9 %copy-start = (bf16[64,2,1,2048]{0,1,3,2:T(2,128)(2,1)S(1)}, bf16[64,2,1,2048]{0,1,3,2:T(2,128)(2,1)}, u32[]{:S(2)}) copy-start(bf16[64,2,1,2048]{0,1,3,2:T(2,128)(2,1)} %copy.58) | copy-start | bytes 1572868
  94.3 4.8 %copy-start.1 = (bf16[64,2,1,2048]{0,1,3,2:T(2,128)(2,1)S(1)}, bf16[64,2,1,2048]{0,1,3,2:T(2,128)(2,1)}, u32[]{:S(2)}) copy-start(bf16[64,2,1,2048]{0,1,3,2:T(2,128)(2,1)} %copy.58) | copy-start | bytes 1572868
  116.1 5.0 %copy-start.2 = (f32[384,2048]{1,0:T(8,128)S(1)}, f32[384,2048]{1,0:T(8,128)}, u32[]{:S(2)}) copy-start(f32[384,2048]{1,0:T(8,128)} %concatenate.25) | copy-start | bytes 9437188
Sparse Core Ops, SparseCore 0:
  21.3 38.2 all-gather.1
  129.3 19.2 reduce-scatter.1

commit v2 on v1

--- a/solution.py
+++ b/solution.py
@@ -3,6 +3,8 @@
 import jax
 import jax.numpy as jnp
 from jax import lax
+from jax.experimental import pallas as pl
+from jax.experimental.pallas import tpu as pltpu
 from jax.sharding import PartitionSpec as P
 
 NSAMP = 32768
@@ -11,6 +13,7 @@
 
 
 EPSILON = 1e-06
+MESH = pl.DeviceIdType.MESH
 
 
 def padded_2(cells, sides, width):
@@ -135,8 +138,333 @@
     )
 
 
+CHUNKS = 4
+STEP = 128
+
+
+def sincos(residue):
+    quadrant = (residue + NSAMP // 8) >> (NSAMP // 4).bit_length() - 1
+    x = (residue - quadrant * (NSAMP // 4)).astype(jnp.float32) * (2.0 * math.pi / NSAMP)
+    y = x * x
+    s = x * (1.0 + y * (-1.0 / 6 + y * (1.0 / 120 + y * (-1.0 / 5040 + y * (1.0 / 362880)))))
+    c = 1.0 + y * (-0.5 + y * (1.0 / 24 + y * (-1.0 / 720 + y * (1.0 / 40320))))
+    odd = (quadrant & 1) == 1
+    sine = jnp.where(odd, c, s)
+    cosine = jnp.where(odd, s, c)
+    sine = jnp.where((quadrant & 2) == 2, -sine, sine)
+    cosine = jnp.where(((quadrant + 1) & 2) == 2, -cosine, cosine)
+    return cosine, sine
+
+
+def kernel(
+    x_ref, off_ref, dead_ref, pick_ref, o_ref,
+    raw, amp, chan, panel, table, rows, ca, sa, cb, sb,
+    raw_sem, send, recv,
+):
+    half = x_ref.shape[1]
+    bins = 2 * half
+    part = bins // CHUNKS
+    lags = o_ref.shape[1]
+    w = lax.axis_index("wide")
+    n = lax.axis_index("narrow")
+    z = w // 4
+    x = (w // 2) % 2
+    c = w % 2
+    rank = z + n * (3 - 2 * z)
+    up_z = z + 1 - 2 * n
+    down_z = z - 1 + 2 * n
+
+    def device(zv, xv, cv):
+        return {"wide": zv * 4 + xv * 2 + cv, "narrow": n}
+
+    up, down = device(up_z, x, c), device(down_z, x, c)
+    x_peer, core_peer = device(z, 1 - x, c), device(z, x, 1 - c)
+    y_peer = {"wide": w, "narrow": 1 - n}
+
+    def slot(role, xv, cv):
+        zl = n if role == 0 else 1 - n
+        return zl * 4 + xv * 2 + cv
+
+    barrier = pltpu.get_barrier_semaphore()
+    for peer in (y_peer, x_peer, core_peer):
+        pl.semaphore_signal(barrier, inc=1, device_id=peer, device_id_type=MESH)
+
+    @pl.when(rank < 3)
+    def _():
+        pl.semaphore_signal(barrier, inc=1, device_id=up, device_id_type=MESH)
+
+    @pl.when(rank > 0)
+    def _():
+        pl.semaphore_signal(barrier, inc=1, device_id=down, device_id_type=MESH)
+
+    pl.semaphore_wait(barrier, 3 + (rank + 2) // 3 + (5 - rank) // 3)
+
+    raw_copy = pltpu.make_async_remote_copy(
+        src_ref=x_ref,
+        dst_ref=raw.at[n],
+        send_sem=raw_sem.at[0],
+        recv_sem=raw_sem.at[1],
+        device_id=y_peer,
+        device_id_type=MESH,
+    )
+    raw_copy.start()
+    raw[n] = x_ref[...]
+
+    def lag_steps(count):
+        lag = lax.broadcasted_iota(jnp.int32, (count, lags), 1)
+        return lag + (NSAMP - lags // 2), lax.broadcasted_iota(jnp.int32, (count, lags), 0)
+
+    steps, at = lag_steps(bins // STEP)
+    ca[...], sa[...] = sincos((steps * at * STEP) & (NSAMP - 1))
+    steps, at = lag_steps(STEP)
+    cb[...], sb[...] = sincos((steps * (at + 1)) & (NSAMP - 1))
+
+    def table_step(a, carry):
+        c1 = ca[pl.ds(a, 1), :]
+        s1 = sa[pl.ds(a, 1), :]
+        for r in range(0, STEP, 16):
+            c2 = cb[r : r + 16, :]
+            s2 = sb[r : r + 16, :]
+            top = pl.ds(pl.multiple_of(a * 2 * STEP + r, 16), 16)
+            low = pl.ds(pl.multiple_of(a * 2 * STEP + STEP + r, 16), 16)
+            table[top, :] = (c1 * c2 - s1 * s2).astype(jnp.bfloat16)
+            table[low, :] = (-s1 * c2 - c1 * s2).astype(jnp.bfloat16)
+        return carry
+
+    lax.fori_loop(0, bins // STEP, table_step, 0)
+
+    raw_copy.wait()
+    zeros = jnp.zeros((32, STEP), jnp.bfloat16)
+    amp[:, 0:STEP] = zeros
+    amp[:, STEP + bins : 2 * STEP + bins] = zeros
+    for h in range(2):
+        re = raw[h, 0:16, :].astype(jnp.float32)
+        im = raw[h, 16:32, :].astype(jnp.float32)
+        size = jnp.sqrt(re * re + im * im)
+        high = size.astype(jnp.bfloat16)
+        cols = pl.ds(STEP + h * half, half)
+        amp[0:16, cols] = high
+        amp[16:32, cols] = (size - high.astype(jnp.float32)).astype(jnp.bfloat16)
+
+    ahead = lax.broadcasted_iota(jnp.int32, (3 * STEP, STEP), 0) - STEP
+    ahead = ahead - lax.broadcasted_iota(jnp.int32, (3 * STEP, STEP), 1)
+    band = jnp.where(jnp.abs(ahead) <= SMOOTH, 1.0, 0.0).astype(jnp.bfloat16)
+
+    def remote(q, at_slot, kind, target):
+        return pltpu.make_async_remote_copy(
+            src_ref=panel.at[q, at_slot],
+            dst_ref=panel.at[q, at_slot],
+            send_sem=send.at[q, kind],
+            recv_sem=recv.at[q, at_slot],
+            device_id=target,
+            device_id_type=MESH,
+        )
+
+    def spread(q, role):
+        remote(q, slot(role, x, c), 4 + role, x_peer).start()
+        remote(q, slot(role, x, c), 6 + role, core_peer).start()
+
+    def arrived(q, at_slot):
+        remote(q, at_slot, 0, core_peer).wait_recv()
+
+    def whiten(q):
+        blocks = part // STEP
+        lhs = jnp.concatenate(
+            [amp[:, (q * blocks + b) * STEP : (q * blocks + b + 3) * STEP] for b in range(blocks)],
+            axis=0,
+        )
+        sums = jnp.dot(lhs, band, preferred_element_type=jnp.float32)
+        windowed = jnp.concatenate(
+            [sums[b * 32 : b * 32 + 16] + sums[b * 32 + 16 : b * 32 + 32] for b in range(blocks)],
+            axis=1,
+        )
+        h, start = q * part // half, q * part % half
+        re = raw[h, 0:16, start : start + part].astype(jnp.float32)
+        im = raw[h, 16:32, start : start + part].astype(jnp.float32)
+        f = lax.broadcasted_iota(jnp.int32, (16, part), 1) + q * part
+        counts = jnp.minimum(f + SMOOTH, bins - 1) - jnp.maximum(f - SMOOTH, 0) + 1
+        smoothed = windowed / counts.astype(jnp.float32) + EPSILON
+        cosine, sine = sincos(((f + 1) * off_ref[:, 0:1]) & (NSAMP - 1))
+        scale = dead_ref[:, 0:1] / smoothed
+        white = jnp.concatenate(
+            [
+                ((re * cosine - im * sine) * scale).astype(jnp.bfloat16),
+                ((re * sine + im * cosine) * scale).astype(jnp.bfloat16),
+            ],
+            axis=0,
+        )
+        picked = jnp.dot(pick_ref[...], white, preferred_element_type=jnp.float32)
+        chan[q] = picked[16:]
+        mine = picked[0:16].astype(jnp.bfloat16)
+
+        @pl.when(rank == 0)
+        def _():
+            panel[q, slot(0, x, c)] = mine
+            remote(q, slot(0, x, c), 0, up).start()
+            spread(q, 0)
+
+        @pl.when(rank == 1)
+        def _():
+            panel[q, slot(1, x, c)] = mine
+            remote(q, slot(1, x, c), 0, up).start()
+            remote(q, slot(1, x, c), 1, down).start()
+            spread(q, 1)
+
+    def along_z(q):
+        @pl.when(rank > 0)
+        def _():
+            arrived(q, slot(0, x, c))
+
+            @pl.when(rank < 3)
+            def _():
+                remote(q, slot(0, x, c), 2, up).start()
+
+            spread(q, 0)
+
+        @pl.when(rank != 1)
+        def _():
+            arrived(q, slot(1, x, c))
+
+            @pl.when(rank == 2)
+            def _():
+                remote(q, slot(1, x, c), 3, up).start()
+
+            spread(q, 1)
+
+    def along_x(q):
+        for role in range(2):
+            arrived(q, slot(role, 1 - x, c))
+            remote(q, slot(role, 1 - x, c), 8 + role, core_peer).start()
+
+    def correlate(q):
+        for role in range(2):
+            for xv in range(2):
+                arrived(q, slot(role, xv, 1 - c))
+        first = lax.broadcasted_iota(jnp.int32, (8, STEP), 0) < 4
+        norm = 1.0 / math.sqrt(2)
+
+        def cross(a, carry):
+            lanes = pl.ds(pl.multiple_of(a * STEP, STEP), STEP)
+            source = [panel[q, b, :, lanes].astype(jnp.float32) for b in range(8)]
+            for ch in range(6):
+                own = chan[q, ch * 16 : ch * 16 + 16, lanes]
+                cr, ci = own[0:8], own[8:16]
+                for imag in range(2):
+                    terms = []
+                    for b in range(8):
+                        sr, si = source[b][0:8], source[b][8:16]
+                        terms.append(sr * ci - si * cr if imag else sr * cr + si * ci)
+                    pairs = []
+                    for b in range(0, 8, 2):
+                        keep = jnp.where(first, terms[b], terms[b + 1])
+                        move = jnp.where(first, terms[b + 1], terms[b])
+                        pairs.append(keep + pltpu.roll(move, 4, 0))
+                    joined = jnp.concatenate(pairs, axis=0) * norm
+                    cols = pl.ds(pl.multiple_of((2 * a + imag) * STEP, STEP), STEP)
+                    rows[ch * 32 : ch * 32 + 32, cols] = joined.astype(jnp.bfloat16)
+            return carry
+
+        lax.fori_loop(0, part // STEP, cross, 0)
+        product = jnp.dot(
+            rows[...],
+            table[q * 2 * part : (q + 1) * 2 * part, :],
+            preferred_element_type=jnp.float32,
+        ) * (1.0 / math.sqrt(bins))
+        if q == 0:
+            o_ref[...] = product
+        else:
+            o_ref[...] += product
+
+    for q in range(CHUNKS):
+        whiten(q)
+    for t in range(CHUNKS + 2):
+        if t < CHUNKS:
+            along_z(t)
+        if 0 <= t - 1 < CHUNKS:
+            along_x(t - 1)
+        if 0 <= t - 2:
+            correlate(t - 2)
+
+    for q in range(CHUNKS):
+        @pl.when(rank < 2)
+        def _():
+            remote(q, 0, 0, core_peer).wait_send()
+
+        @pl.when(rank == 1)
+        def _():
+            remote(q, 0, 1, core_peer).wait_send()
+
+        @pl.when((rank + 1) // 2 == 1)
+        def _():
+            remote(q, 0, 2, core_peer).wait_send()
+
+        @pl.when(rank == 2)
+        def _():
+            remote(q, 0, 3, core_peer).wait_send()
+
+        for kind in range(4, 10):
+            remote(q, 0, kind, core_peer).wait_send()
+
+
+def fused_body(spectra, dead_mask, seg_offsets, src_index):
+    ch_count, seg_count, _, half = spectra.shape
+    bins = 2 * half
+    wide_pos = lax.axis_index("wide")
+    spare = 8 - ch_count
+    cells = jnp.pad(spectra.transpose(2, 1, 0, 3), ((0, 0), (0, 0), (0, spare), (0, 0)))
+    cells = cells.reshape(32, half)
+    off = jnp.pad(seg_offsets.T, ((0, 0), (0, spare))).reshape(16, 1)
+    dead = jnp.pad(dead_mask.astype(jnp.float32), (0, spare))
+    dead = jnp.concatenate([dead, dead]).reshape(16, 1)
+    own = lax.dynamic_slice_in_dim(src_index, wide_pos * 4, 4) - wide_pos * ch_count
+    plane = jnp.arange(4, dtype=jnp.int32) * 8
+    head = (plane[:, None] + own[None, :]).reshape(16)
+    tail = jnp.arange(ch_count, dtype=jnp.int32)[:, None, None] + plane[None, :, None]
+    tail = jnp.broadcast_to(tail, (ch_count, 4, 4)).reshape(ch_count * 16)
+    wanted = jnp.concatenate([head, tail])
+    pick = (wanted[:, None] == jnp.arange(32, dtype=jnp.int32)[None, :]).astype(jnp.bfloat16)
+    shares = src_index.shape[0] // 2
+    vmem = pl.BlockSpec(memory_space=pltpu.VMEM)
+    f32, bf16 = jnp.float32, jnp.bfloat16
+    result = pl.pallas_call(
+        kernel,
+        out_shape=jax.ShapeDtypeStruct((ch_count * shares, LAGS), f32),
+        in_specs=[vmem] * 4,
+        out_specs=vmem,
+        scratch_shapes=[
+            pltpu.VMEM((2, 32, half), bf16),
+            pltpu.VMEM((32, bins + 2 * STEP), bf16),
+            pltpu.VMEM((CHUNKS, ch_count * 16, bins // CHUNKS), f32),
+            pltpu.VMEM((CHUNKS, 8, 16, bins // CHUNKS), bf16),
+            pltpu.VMEM((2 * bins, LAGS), bf16),
+            pltpu.VMEM((ch_count * shares, 2 * bins // CHUNKS), bf16),
+            pltpu.VMEM((bins // STEP, LAGS), f32),
+            pltpu.VMEM((bins // STEP, LAGS), f32),
+            pltpu.VMEM((STEP, LAGS), f32),
+            pltpu.VMEM((STEP, LAGS), f32),
+            pltpu.SemaphoreType.DMA((2,)),
+            pltpu.SemaphoreType.DMA((CHUNKS, 10)),
+            pltpu.SemaphoreType.DMA((CHUNKS, 8)),
+        ],
+        compiler_params=pltpu.CompilerParams(
+            collective_id=0, has_side_effects=True, vmem_limit_bytes=40 * 1024 * 1024
+        ),
+    )(
+        cells,
+        jnp.broadcast_to(off, (16, STEP)),
+        jnp.broadcast_to(dead, (16, STEP)),
+        pick,
+    )
+    return result.reshape(ch_count, shares, LAGS).transpose(1, 0, 2)
+
+
 def solution(mesh):
     placed = (P("wide", None, None, "narrow"), P("wide"), P("wide", None), P())
+    fits = mesh.shape["wide"] == 16 and mesh.shape["narrow"] == 2
     return jax.shard_map(
-        body, mesh=mesh, in_specs=placed, out_specs=P("narrow", "wide", None), check_vma=False
-    )
+        fused_body if fits else body,
+        mesh=mesh,
+        in_specs=placed,
+        out_specs=P("narrow", "wide", None),
+        check_vma=False,
+    )

time: 158 us -> 33.2 us (0.21)
  the two profiles are of different devices: /device:TPU:0 before, /device:TPU:5 now
where the time goes in v2:
time: 33.2 us; the launch traced here: 33 us
  Pallas kernels  29.2 us (88%)
  local copies, waits for them, and re-layouts  2.02 us (6%)
  other arithmetic  1.74 us (5%)
    pallas_call x1, Pallas kernels, fused_body(): pl.pallas_call(kernel, out_shape=jax.ShapeDtypeStruct((ch_count * shares,...  29.2 us
    unnamed x4, local copies, waits for them, and re-layouts  0.81 us
    sub x1, other arithmetic, fused_body(): lax.dynamic_slice_in_dim(src_index, wide_pos * 4, 4) - wide_pos * ch_count  0.76 us
    pad x1, local copies, waits for them, and re-layouts, fused_body(): off = jnp.pad(seg_offsets.T, ((0, 0), (0, spare))).reshape(16, 1)  0.68 us

profile of v2, /device:TPU:5, one launch (start us, length us, event | category | flops | bytes accessed | tf_op | source)
XLA Modules:
  0.0 33.0 jit_solution(255753758384696417)
XLA Ops:
  0.0 0.0 copy-start
  0.0 0.8 %dynamic-slice_subtract_fusion = (s32[4]{0:T(128)S(1)}, s32[4]{0:T(128)S(1)}) fusion(s32[64]{0:T(128)} %param.7, s32[]{:T(128)S(6)} %select_n.3, s32[]{:T(128)S(6)} %mul.21), kind=kLoop, calls=%fused_computation.6 | loop fusion | flops 8 | bytes 56 | tf_op jit(solution)/shard_map/sub | solution.py:419
  0.8 0.7 %convert_element_type.10 = f32[6]{0:T(128)S(1)} convert(s32[6]{0:T(128)} %param.5) | non-fusion elementwise | flops 6 | bytes 48 | tf_op jit(solution)/shard_map/convert_element_type | solution.py:417
  1.4 0.1 pad_maximum_fusion
  1.5 0.7 %pad.13 = s32[2,8]{1,0:T(2,128)S(1)} pad(s32[2,6]{1,0:T(2,128)} %bitcast.9, s32[]{:T(128)} %constant.5.clone.1), padding=0_0x0_2 | pad | bytes 116 | tf_op jit(solution)/shard_map/jit(_pad)/pad | solution.py:416
  2.2 0.1 broadcast_in_dim.8
  2.3 0.1 broadcast_add_fusion
  2.3 0.1 add.48
  2.4 0.1 broadcast_in_dim.9.off_ref
  2.5 0.1 broadcast_in_dim.10.dead_ref
  2.6 0.1 broadcast_in_dim.11
  2.6 0.1 reshape.51
  2.8 0.1 pad_add_fusion
  2.8 0.1 fusion.pick_ref
  2.9 0.0 copy-done
  2.9 0.1 copy.7
  3.0 29.2 %shard_map.46 = f32[192,512]{1,0:T(8,128)S(1)} custom-call(bf16[32,2048]{1,0:T(8,128)(2,1)S(1)} %bitcast.7, s32[16,128]{1,0:T(8,128)S(1)} %broadcast_in_dim.9.off_ref, f32[16,128]{1,0:T(8,128)S(1)} %broadcast_in_dim.10.dead_ref, bf16[112,32]{1,0:T(8,128)(2,1)S(1)} %fusion.pick_ref), custom_call_target="tpu_custom_call" | custom-call | tf_op jit(solution)/shard_map/pallas_call | solution.py:429
  32.3 0.7 %copy.9 = f32[32,6,512]{2,0,1:T(8,128)} copy(f32[32,6,512]{2,0,1:T(8,128)S(1)} %bitcast.6) | data formatting | bytes 786432
  (3 shorter events, 0.0 us)
Async XLA Ops:
  0.0 2.9 %copy-start = (bf16[6,2,2,2048]{3,2,1,0:T(2,128)(2,1)S(1)}, bf16[6,2,2,2048]{3,2,1,0:T(2,128)(2,1)}, u32[]{:S(2)}) copy-start(bf16[6,2,2,2048]{3,2,1,0:T(2,128)(2,1)} %param.4) | copy-start | bytes 294916

commit v3 on v2

--- a/solution.py
+++ b/solution.py
@@ -157,9 +157,9 @@
 
 
 def kernel(
-    x_ref, off_ref, dead_ref, pick_ref, o_ref,
-    raw, amp, chan, panel, table, rows, ca, sa, cb, sb,
-    raw_sem, send, recv,
+    x_ref, off_ref, dead_ref, src_ref, o_ref,
+    amp, halo, white, chan, panel, relay, table, rows, ca, sa, cb, sb,
+    halo_sem, send, recv, relay_recv, white_recv,
 ):
     half = x_ref.shape[1]
     bins = 2 * half
@@ -182,8 +182,13 @@
     y_peer = {"wide": w, "narrow": 1 - n}
 
     def slot(role, xv, cv):
-        zl = n if role == 0 else 1 - n
-        return zl * 4 + xv * 2 + cv
+        return (n if role == 0 else 1 - n) * 4 + xv * 2 + cv
+
+    def peer_slot(role):
+        return (1 - n if role == 0 else n) * 4 + x * 2 + c
+
+    def chunk(q):
+        return q + n * (3 - 2 * q)
 
     barrier = pltpu.get_barrier_semaphore()
     for peer in (y_peer, x_peer, core_peer):
@@ -197,66 +202,91 @@
     def _():
         pl.semaphore_signal(barrier, inc=1, device_id=down, device_id_type=MESH)
 
+    def amplitude(cells):
+        re = cells[0:16].astype(jnp.float32)
+        im = cells[16:32].astype(jnp.float32)
+        size = jnp.sqrt(re * re + im * im)
+        high = size.astype(jnp.bfloat16)
+        return high, (size - high.astype(jnp.float32)).astype(jnp.bfloat16)
+
+    zeros = jnp.zeros((32, STEP), jnp.bfloat16)
+    amp[:, 0:STEP] = zeros
+    amp[:, STEP + half : 2 * STEP + half] = zeros
+    high, low = amplitude(x_ref[...])
+    amp[0:16, STEP : STEP + half] = high
+    amp[16:32, STEP : STEP + half] = low
+
+    ahead = lax.broadcasted_iota(jnp.int32, (3 * STEP, STEP), 0) - STEP
+    ahead = ahead - lax.broadcasted_iota(jnp.int32, (3 * STEP, STEP), 1)
+    band = jnp.where(jnp.abs(ahead) <= SMOOTH, 1.0, 0.0).astype(jnp.bfloat16)
+
+    line = lax.broadcasted_iota(jnp.int32, (16, STEP), 0)
+    offsets = jnp.zeros((16, STEP), jnp.int32)
+    live = jnp.zeros((16, STEP), jnp.int32)
+    for ch in range(6):
+        live = jnp.where((line & 7) == ch, dead_ref[ch], live)
+        for k in range(2):
+            offsets = jnp.where(line == k * 8 + ch, off_ref[k, ch], offsets)
+    offsets = offsets[:, 0:1]
+    live = live[:, 0:1].astype(jnp.float32)
+    line = lax.broadcasted_iota(jnp.int32, (112, 32), 0)
+    wanted = (line >> 4) - 1
+    for r in range(4):
+        wanted = jnp.where((line & 3) + (line >> 4) * 4 == r, src_ref[w * 4 + r] - w * 6, wanted)
+    wanted = wanted + ((line & 15) >> 2) * 8
+    column = lax.broadcasted_iota(jnp.int32, (112, 32), 1)
+    pick = jnp.where(wanted == column, 1.0, 0.0).astype(jnp.bfloat16)
+
     pl.semaphore_wait(barrier, 3 + (rank + 2) // 3 + (5 - rank) // 3)
 
-    raw_copy = pltpu.make_async_remote_copy(
-        src_ref=x_ref,
-        dst_ref=raw.at[n],
-        send_sem=raw_sem.at[0],
-        recv_sem=raw_sem.at[1],
+    edge = pl.ds(pl.multiple_of((1 - n) * (half - STEP), STEP), STEP)
+    halo_copy = pltpu.make_async_remote_copy(
+        src_ref=x_ref.at[:, edge],
+        dst_ref=halo,
+        send_sem=halo_sem.at[0],
+        recv_sem=halo_sem.at[1],
         device_id=y_peer,
         device_id_type=MESH,
     )
-    raw_copy.start()
-    raw[n] = x_ref[...]
-
-    def lag_steps(count):
-        lag = lax.broadcasted_iota(jnp.int32, (count, lags), 1)
-        return lag + (NSAMP - lags // 2), lax.broadcasted_iota(jnp.int32, (count, lags), 0)
-
-    steps, at = lag_steps(bins // STEP)
-    ca[...], sa[...] = sincos((steps * at * STEP) & (NSAMP - 1))
-    steps, at = lag_steps(STEP)
-    cb[...], sb[...] = sincos((steps * (at + 1)) & (NSAMP - 1))
-
-    def table_step(a, carry):
-        c1 = ca[pl.ds(a, 1), :]
-        s1 = sa[pl.ds(a, 1), :]
-        for r in range(0, STEP, 16):
-            c2 = cb[r : r + 16, :]
-            s2 = sb[r : r + 16, :]
-            top = pl.ds(pl.multiple_of(a * 2 * STEP + r, 16), 16)
-            low = pl.ds(pl.multiple_of(a * 2 * STEP + STEP + r, 16), 16)
-            table[top, :] = (c1 * c2 - s1 * s2).astype(jnp.bfloat16)
-            table[low, :] = (-s1 * c2 - c1 * s2).astype(jnp.bfloat16)
-        return carry
-
-    lax.fori_loop(0, bins // STEP, table_step, 0)
-
-    raw_copy.wait()
-    zeros = jnp.zeros((32, STEP), jnp.bfloat16)
-    amp[:, 0:STEP] = zeros
-    amp[:, STEP + bins : 2 * STEP + bins] = zeros
-    for h in range(2):
-        re = raw[h, 0:16, :].astype(jnp.float32)
-        im = raw[h, 16:32, :].astype(jnp.float32)
-        size = jnp.sqrt(re * re + im * im)
-        high = size.astype(jnp.bfloat16)
-        cols = pl.ds(STEP + h * half, half)
-        amp[0:16, cols] = high
-        amp[16:32, cols] = (size - high.astype(jnp.float32)).astype(jnp.bfloat16)
-
-    ahead = lax.broadcasted_iota(jnp.int32, (3 * STEP, STEP), 0) - STEP
-    ahead = ahead - lax.broadcasted_iota(jnp.int32, (3 * STEP, STEP), 1)
-    band = jnp.where(jnp.abs(ahead) <= SMOOTH, 1.0, 0.0).astype(jnp.bfloat16)
+    halo_copy.start()
 
     def remote(q, at_slot, kind, target):
         return pltpu.make_async_remote_copy(
-            src_ref=panel.at[q, at_slot],
-            dst_ref=panel.at[q, at_slot],
+            src_ref=panel.at[chunk(q), at_slot],
+            dst_ref=panel.at[chunk(q), at_slot],
             send_sem=send.at[q, kind],
-            recv_sem=recv.at[q, at_slot],
+            recv_sem=recv.at[chunk(q), at_slot],
             device_id=target,
+            device_id_type=MESH,
+        )
+
+    def relayed(q, role):
+        return pltpu.make_async_remote_copy(
+            src_ref=relay.at[q, role],
+            dst_ref=relay.at[q, role],
+            send_sem=send.at[q, 10 + role],
+            recv_sem=relay_recv.at[q, role],
+            device_id=down,
+            device_id_type=MESH,
+        )
+
+    def crossing(q, role):
+        return pltpu.make_async_remote_copy(
+            src_ref=relay.at[q, role],
+            dst_ref=panel.at[chunk(q), peer_slot(role)],
+            send_sem=send.at[q, 12 + role],
+            recv_sem=recv.at[chunk(q), peer_slot(role)],
+            device_id=y_peer,
+            device_id_type=MESH,
+        )
+
+    def white_copy(q, g):
+        return pltpu.make_async_remote_copy(
+            src_ref=white.at[g],
+            dst_ref=white.at[g],
+            send_sem=send.at[q, 14],
+            recv_sem=white_recv.at[g],
+            device_id=y_peer,
             device_id_type=MESH,
         )
 
@@ -267,10 +297,20 @@
     def arrived(q, at_slot):
         remote(q, at_slot, 0, core_peer).wait_recv()
 
+    def choose(q, cells):
+        picked = jnp.dot(pick, cells, preferred_element_type=jnp.float32)
+        chan[chunk(q)] = picked[16:]
+        return picked[0:16].astype(jnp.bfloat16)
+
     def whiten(q):
         blocks = part // STEP
+        g = chunk(q)
+        start = (g - 2 * n) * part
         lhs = jnp.concatenate(
-            [amp[:, (q * blocks + b) * STEP : (q * blocks + b + 3) * STEP] for b in range(blocks)],
+            [
+                amp[:, pl.ds(pl.multiple_of(start + b * STEP, STEP), 3 * STEP)]
+                for b in range(blocks)
+            ],
             axis=0,
         )
         sums = jnp.dot(lhs, band, preferred_element_type=jnp.float32)
@@ -278,76 +318,163 @@
             [sums[b * 32 : b * 32 + 16] + sums[b * 32 + 16 : b * 32 + 32] for b in range(blocks)],
             axis=1,
         )
-        h, start = q * part // half, q * part % half
-        re = raw[h, 0:16, start : start + part].astype(jnp.float32)
-        im = raw[h, 16:32, start : start + part].astype(jnp.float32)
-        f = lax.broadcasted_iota(jnp.int32, (16, part), 1) + q * part
+        lanes = pl.ds(pl.multiple_of(start, STEP), part)
+        re = x_ref[0:16, lanes].astype(jnp.float32)
+        im = x_ref[16:32, lanes].astype(jnp.float32)
+        f = lax.broadcasted_iota(jnp.int32, (16, part), 1) + g * part
         counts = jnp.minimum(f + SMOOTH, bins - 1) - jnp.maximum(f - SMOOTH, 0) + 1
         smoothed = windowed / counts.astype(jnp.float32) + EPSILON
-        cosine, sine = sincos(((f + 1) * off_ref[:, 0:1]) & (NSAMP - 1))
-        scale = dead_ref[:, 0:1] / smoothed
-        white = jnp.concatenate(
+        cosine, sine = sincos(((f + 1) * offsets) & (NSAMP - 1))
+        scale = live / smoothed
+        cells = jnp.concatenate(
             [
                 ((re * cosine - im * sine) * scale).astype(jnp.bfloat16),
                 ((re * sine + im * cosine) * scale).astype(jnp.bfloat16),
             ],
             axis=0,
         )
-        picked = jnp.dot(pick_ref[...], white, preferred_element_type=jnp.float32)
-        chan[q] = picked[16:]
-        mine = picked[0:16].astype(jnp.bfloat16)
+        white[g] = cells
+        mine = choose(q, cells)
 
         @pl.when(rank == 0)
         def _():
-            panel[q, slot(0, x, c)] = mine
+            panel[g, slot(0, x, c)] = mine
             remote(q, slot(0, x, c), 0, up).start()
             spread(q, 0)
 
         @pl.when(rank == 1)
         def _():
-            panel[q, slot(1, x, c)] = mine
+            panel[g, slot(1, x, c)] = mine
             remote(q, slot(1, x, c), 0, up).start()
             remote(q, slot(1, x, c), 1, down).start()
             spread(q, 1)
 
+        @pl.when(rank == 2)
+        def _():
+            relay[q, 1] = mine
+            relayed(q, 1).start()
+
+        @pl.when(rank == 3)
+        def _():
+            relay[q, 0] = mine
+            relayed(q, 0).start()
+
+        white_copy(q, g).start()
+
     def along_z(q):
-        @pl.when(rank > 0)
+        @pl.when(rank == 0)
+        def _():
+            arrived(q, slot(1, x, c))
+            spread(q, 1)
+            for role in range(2):
+                relayed(q, role).wait_recv()
+                crossing(q, role).start()
+
+        @pl.when(rank == 1)
         def _():
             arrived(q, slot(0, x, c))
-
-            @pl.when(rank < 3)
-            def _():
-                remote(q, slot(0, x, c), 2, up).start()
-
+            remote(q, slot(0, x, c), 2, up).start()
             spread(q, 0)
-
-        @pl.when(rank != 1)
+            for role in (1, 0):
+                relayed(q, role).wait_recv()
+                relayed(q, role).start()
+                crossing(q, role).start()
+
+        @pl.when(rank == 2)
+        def _():
+            relayed(q, 0).wait_recv()
+            relayed(q, 0).start()
+            for role in (1, 0):
+                arrived(q, slot(role, x, c))
+                remote(q, slot(role, x, c), 2 + role, up).start()
+                spread(q, role)
+
+        @pl.when(rank == 3)
+        def _():
+            for role in (1, 0):
+                arrived(q, slot(role, x, c))
+                spread(q, role)
+
+    def along_y(q):
+        g = chunk(q)
+        white_copy(q, g).wait_recv()
+        mine = choose(q, white[g])
+
+        @pl.when(rank == 0)
+        def _():
+            panel[g, slot(0, x, c)] = mine
+            remote(q, slot(0, x, c), 0, up).start()
+            spread(q, 0)
+
+        @pl.when(rank == 1)
+        def _():
+            panel[g, slot(1, x, c)] = mine
+            remote(q, slot(1, x, c), 1, down).start()
+            spread(q, 1)
+
+    def after_y(q):
+        @pl.when(rank == 0)
         def _():
             arrived(q, slot(1, x, c))
-
-            @pl.when(rank == 2)
-            def _():
-                remote(q, slot(1, x, c), 3, up).start()
-
             spread(q, 1)
+
+        @pl.when(rank == 1)
+        def _():
+            arrived(q, slot(0, x, c))
+            spread(q, 0)
+
+        @pl.when(rank > 1)
+        def _():
+            for role in (1, 0):
+                arrived(q, slot(role, x, c))
+                spread(q, role)
 
     def along_x(q):
         for role in range(2):
             arrived(q, slot(role, 1 - x, c))
             remote(q, slot(role, 1 - x, c), 8 + role, core_peer).start()
 
+    def lag_steps(count):
+        lag = lax.broadcasted_iota(jnp.int32, (count, lags), 1)
+        return lag + (NSAMP - lags // 2), lax.broadcasted_iota(jnp.int32, (count, lags), 0)
+
+    def table_base():
+        steps, at = lag_steps(bins // STEP)
+        ca[...], sa[...] = sincos((steps * at * STEP) & (NSAMP - 1))
+        steps, at = lag_steps(STEP)
+        cb[...], sb[...] = sincos((steps * (at + 1)) & (NSAMP - 1))
+
+    def table_part(q):
+        first = chunk(q) * (part // STEP)
+
+        def table_step(i, carry):
+            a = first + i
+            c1 = ca[pl.ds(a, 1), :]
+            s1 = sa[pl.ds(a, 1), :]
+            for r in range(0, STEP, 16):
+                c2 = cb[r : r + 16, :]
+                s2 = sb[r : r + 16, :]
+                top = pl.ds(pl.multiple_of(a * 2 * STEP + r, 16), 16)
+                low = pl.ds(pl.multiple_of(a * 2 * STEP + STEP + r, 16), 16)
+                table[top, :] = (c1 * c2 - s1 * s2).astype(jnp.bfloat16)
+                table[low, :] = (-s1 * c2 - c1 * s2).astype(jnp.bfloat16)
+            return carry
+
+        lax.fori_loop(0, part // STEP, table_step, 0)
+
     def correlate(q):
         for role in range(2):
             for xv in range(2):
                 arrived(q, slot(role, xv, 1 - c))
+        g = chunk(q)
         first = lax.broadcasted_iota(jnp.int32, (8, STEP), 0) < 4
         norm = 1.0 / math.sqrt(2)
 
         def cross(a, carry):
             lanes = pl.ds(pl.multiple_of(a * STEP, STEP), STEP)
-            source = [panel[q, b, :, lanes].astype(jnp.float32) for b in range(8)]
+            source = [panel[g, b, :, lanes].astype(jnp.float32) for b in range(8)]
             for ch in range(6):
-                own = chan[q, ch * 16 : ch * 16 + 16, lanes]
+                own = chan[g, ch * 16 : ch * 16 + 16, lanes]
                 cr, ci = own[0:8], own[8:16]
                 for imag in range(2):
                     terms = []
@@ -367,7 +494,7 @@
         lax.fori_loop(0, part // STEP, cross, 0)
         product = jnp.dot(
             rows[...],
-            table[q * 2 * part : (q + 1) * 2 * part, :],
+            table[pl.ds(pl.multiple_of(g * 2 * part, 16), 2 * part), :],
             preferred_element_type=jnp.float32,
         ) * (1.0 / math.sqrt(bins))
         if q == 0:
@@ -375,86 +502,104 @@
         else:
             o_ref[...] += product
 
+    whiten(0)
+    table_base()
+    halo_copy.wait()
+    high, low = amplitude(halo[...])
+    edge = pl.ds(pl.multiple_of((1 - n) * (half + STEP), STEP), STEP)
+    amp[0:16, edge] = high
+    amp[16:32, edge] = low
+    whiten(1)
+    along_z(0)
+    table_part(0)
+    along_z(1)
+    along_y(3)
+    along_x(0)
+    table_part(1)
+    along_y(2)
+    after_y(3)
+    along_x(1)
+    correlate(0)
+    after_y(2)
+    along_x(3)
+    table_part(3)
+    correlate(1)
+    along_x(2)
+    table_part(2)
+    correlate(3)
+    correlate(2)
+
+    def sent(q, kind):
+        remote(q, 0, kind, core_peer).wait_send()
+
     for q in range(CHUNKS):
-        whiten(q)
-    for t in range(CHUNKS + 2):
-        if t < CHUNKS:
-            along_z(t)
-        if 0 <= t - 1 < CHUNKS:
-            along_x(t - 1)
-        if 0 <= t - 2:
-            correlate(t - 2)
-
-    for q in range(CHUNKS):
-        @pl.when(rank < 2)
-        def _():
-            remote(q, 0, 0, core_peer).wait_send()
+        own_half = q < 2
+
+        @pl.when(rank == 0)
+        def _():
+            for kind in (0, 12, 13) if own_half else (0,):
+                sent(q, kind)
 
         @pl.when(rank == 1)
         def _():
-            remote(q, 0, 1, core_peer).wait_send()
-
-        @pl.when((rank + 1) // 2 == 1)
-        def _():
-            remote(q, 0, 2, core_peer).wait_send()
-
-        @pl.when(rank == 2)
-        def _():
-            remote(q, 0, 3, core_peer).wait_send()
+            for kind in (0, 1, 2, 10, 11, 12, 13) if own_half else (1,):
+                sent(q, kind)
+
+        if own_half:
+            white_copy(q, chunk(q)).wait_send()
+
+            @pl.when(rank == 2)
+            def _():
+                for kind in (2, 3, 10, 11):
+                    sent(q, kind)
+
+            @pl.when(rank == 3)
+            def _():
+                sent(q, 10)
 
         for kind in range(4, 10):
-            remote(q, 0, kind, core_peer).wait_send()
+            sent(q, kind)
 
 
 def fused_body(spectra, dead_mask, seg_offsets, src_index):
     ch_count, seg_count, _, half = spectra.shape
     bins = 2 * half
-    wide_pos = lax.axis_index("wide")
+    part = bins // CHUNKS
     spare = 8 - ch_count
     cells = jnp.pad(spectra.transpose(2, 1, 0, 3), ((0, 0), (0, 0), (0, spare), (0, 0)))
     cells = cells.reshape(32, half)
-    off = jnp.pad(seg_offsets.T, ((0, 0), (0, spare))).reshape(16, 1)
-    dead = jnp.pad(dead_mask.astype(jnp.float32), (0, spare))
-    dead = jnp.concatenate([dead, dead]).reshape(16, 1)
-    own = lax.dynamic_slice_in_dim(src_index, wide_pos * 4, 4) - wide_pos * ch_count
-    plane = jnp.arange(4, dtype=jnp.int32) * 8
-    head = (plane[:, None] + own[None, :]).reshape(16)
-    tail = jnp.arange(ch_count, dtype=jnp.int32)[:, None, None] + plane[None, :, None]
-    tail = jnp.broadcast_to(tail, (ch_count, 4, 4)).reshape(ch_count * 16)
-    wanted = jnp.concatenate([head, tail])
-    pick = (wanted[:, None] == jnp.arange(32, dtype=jnp.int32)[None, :]).astype(jnp.bfloat16)
     shares = src_index.shape[0] // 2
     vmem = pl.BlockSpec(memory_space=pltpu.VMEM)
+    smem = pl.BlockSpec(memory_space=pltpu.SMEM)
     f32, bf16 = jnp.float32, jnp.bfloat16
     result = pl.pallas_call(
         kernel,
         out_shape=jax.ShapeDtypeStruct((ch_count * shares, LAGS), f32),
-        in_specs=[vmem] * 4,
+        in_specs=[vmem, smem, smem, smem],
         out_specs=vmem,
         scratch_shapes=[
-            pltpu.VMEM((2, 32, half), bf16),
-            pltpu.VMEM((32, bins + 2 * STEP), bf16),
-            pltpu.VMEM((CHUNKS, ch_count * 16, bins // CHUNKS), f32),
-            pltpu.VMEM((CHUNKS, 8, 16, bins // CHUNKS), bf16),
+            pltpu.VMEM((32, half + 2 * STEP), bf16),
+            pltpu.VMEM((32, STEP), bf16),
+            pltpu.VMEM((CHUNKS, 32, part), bf16),
+            pltpu.VMEM((CHUNKS, ch_count * 16, part), f32),
+            pltpu.VMEM((CHUNKS, 8, 16, part), bf16),
+            pltpu.VMEM((2, 2, 16, part), bf16),
             pltpu.VMEM((2 * bins, LAGS), bf16),
-            pltpu.VMEM((ch_count * shares, 2 * bins // CHUNKS), bf16),
+            pltpu.VMEM((ch_count * shares, 2 * part), bf16),
             pltpu.VMEM((bins // STEP, LAGS), f32),
             pltpu.VMEM((bins // STEP, LAGS), f32),
             pltpu.VMEM((STEP, LAGS), f32),
             pltpu.VMEM((STEP, LAGS), f32),
             pltpu.SemaphoreType.DMA((2,)),
-            pltpu.SemaphoreType.DMA((CHUNKS, 10)),
+            pltpu.SemaphoreType.DMA((CHUNKS, 15)),
             pltpu.SemaphoreType.DMA((CHUNKS, 8)),
+            pltpu.SemaphoreType.DMA((2, 2)),
+            pltpu.SemaphoreType.DMA((CHUNKS,)),
         ],
         compiler_params=pltpu.CompilerParams(
             collective_id=0, has_side_effects=True, vmem_limit_bytes=40 * 1024 * 1024
         ),
-    )(
-        cells,
-        jnp.broadcast_to(off, (16, STEP)),
-        jnp.broadcast_to(dead, (16, STEP)),
-        pick,
-    )
+    )(cells, seg_offsets.T, dead_mask, src_index)
     return result.reshape(ch_count, shares, LAGS).transpose(1, 0, 2)
 
 

time: 33.2 us -> 31 us (0.934)
  the two profiles are of different devices: /device:TPU:5 before, /device:TPU:0 now
where the time goes in v3:
time: 31 us; the launch traced here: 30.8 us
  Pallas kernels  28.4 us (92%)
  local copies, waits for them, and re-layouts  2.4 us (8%)
    pallas_call x1, Pallas kernels, fused_body(): pl.pallas_call(kernel, out_shape=jax.ShapeDtypeStruct((ch_count * shares,...  28.4 us
    unnamed x8, local copies, waits for them, and re-layouts  2.37 us

profile of v3, /device:TPU:0, one launch (start us, length us, event | category | flops | bytes accessed | tf_op | source)
XLA Modules:
  0.0 30.8 jit_solution(16997475035196608712)
XLA Ops:
  0.0 1.0 %copy.6 = bf16[2,2,6,2048]{3,2,1,0:T(8,128)(2,1)S(1)} copy(bf16[2,2,6,2048]{3,0,1,2:T(2,128)(2,1)} %bitcast.9) | data formatting | bytes 196608
  1.0 0.0 copy-start.2
  1.0 0.0 copy-start
  1.0 0.0 copy-start.1
  1.0 0.6 %copy-done.2 = s32[64]{0:T(128)S(1)} copy-done((s32[64]{0:T(128)S(1)}, s32[64]{0:T(128)}, u32[]{:S(2)}) %copy-start.2) | copy-done | bytes 280
  1.6 0.1 copy-done
  1.7 0.0 copy-done.1
  1.7 28.4 %shard_map.46 = f32[192,512]{1,0:T(8,128)S(1)} custom-call(bf16[32,2048]{1,0:T(8,128)(2,1)S(1)} %bitcast.7, s32[2,6]{1,0:T(2,128)S(1)} %bitcast.8, s32[6]{0:T(128)S(1)} %copy-done.1, s32[64]{0:T(128)S(1)} %copy-done.2), custom_call_target="tpu_custom_call" | custom-call | tf_op jit(solution)/shard_map/pallas_call | solution.py:575
  30.1 0.7 %copy.8 = f32[32,6,512]{2,0,1:T(8,128)} copy(f32[32,6,512]{2,0,1:T(8,128)S(1)} %bitcast.6) | data formatting | bytes 786432
  (1 shorter events, 0.0 us)
Async XLA Ops:
  1.0 0.7 %copy-start.2 = (s32[64]{0:T(128)S(1)}, s32[64]{0:T(128)}, u32[]{:S(2)}) copy-start(s32[64]{0:T(128)} %src_ref.1) | copy-start | bytes 772
  1.0 0.7 %copy-start = (s32[6,2]{0,1:T(2,128)S(1)}, s32[6,2]{0,1:T(2,128)}, u32[]{:S(2)}) copy-start(s32[6,2]{0,1:T(2,128)} %param.6) | copy-start | bytes 148
  1.0 0.7 %copy-start.1 = (s32[6]{0:T(128)S(1)}, s32[6]{0:T(128)}, u32[]{:S(2)}) copy-start(s32[6]{0:T(128)} %dead_ref.1) | copy-start | bytes 76

commit v4 on v3

--- a/solution.py
+++ b/solution.py
@@ -158,8 +158,8 @@
 
 def kernel(
     x_ref, off_ref, dead_ref, src_ref, o_ref,
-    amp, halo, white, chan, panel, relay, table, rows, ca, sa, cb, sb,
-    halo_sem, send, recv, relay_recv, white_recv,
+    amp, halo, white, chan, panel, table, rows, ca, sa, cb, sb,
+    halo_sem, send, recv, white_recv,
 ):
     half = x_ref.shape[1]
     bins = 2 * half
@@ -171,21 +171,17 @@
     x = (w // 2) % 2
     c = w % 2
     rank = z + n * (3 - 2 * z)
-    up_z = z + 1 - 2 * n
-    down_z = z - 1 + 2 * n
-
     def device(zv, xv, cv):
         return {"wide": zv * 4 + xv * 2 + cv, "narrow": n}
 
-    up, down = device(up_z, x, c), device(down_z, x, c)
+    def ranked(k):
+        return device(k + n * (3 - 2 * k), x, c)
+
     x_peer, core_peer = device(z, 1 - x, c), device(z, x, 1 - c)
     y_peer = {"wide": w, "narrow": 1 - n}
 
     def slot(role, xv, cv):
         return (n if role == 0 else 1 - n) * 4 + xv * 2 + cv
-
-    def peer_slot(role):
-        return (1 - n if role == 0 else n) * 4 + x * 2 + c
 
     def chunk(q):
         return q + n * (3 - 2 * q)
@@ -194,13 +190,13 @@
     for peer in (y_peer, x_peer, core_peer):
         pl.semaphore_signal(barrier, inc=1, device_id=peer, device_id_type=MESH)
 
-    @pl.when(rank < 3)
-    def _():
-        pl.semaphore_signal(barrier, inc=1, device_id=up, device_id_type=MESH)
-
-    @pl.when(rank > 0)
-    def _():
-        pl.semaphore_signal(barrier, inc=1, device_id=down, device_id_type=MESH)
+    for k, others in enumerate(((1, 2), (0, 2), (0, 1, 3), (2,))):
+        @pl.when(rank == k)
+        def _():
+            for other in others:
+                pl.semaphore_signal(
+                    barrier, inc=1, device_id=ranked(other), device_id_type=MESH
+                )
 
     def amplitude(cells):
         re = cells[0:16].astype(jnp.float32)
@@ -237,7 +233,7 @@
     column = lax.broadcasted_iota(jnp.int32, (112, 32), 1)
     pick = jnp.where(wanted == column, 1.0, 0.0).astype(jnp.bfloat16)
 
-    pl.semaphore_wait(barrier, 3 + (rank + 2) // 3 + (5 - rank) // 3)
+    pl.semaphore_wait(barrier, 5 + (rank // 2) * (5 - 2 * rank))
 
     edge = pl.ds(pl.multiple_of((1 - n) * (half - STEP), STEP), STEP)
     halo_copy = pltpu.make_async_remote_copy(
@@ -260,31 +256,11 @@
             device_id_type=MESH,
         )
 
-    def relayed(q, role):
-        return pltpu.make_async_remote_copy(
-            src_ref=relay.at[q, role],
-            dst_ref=relay.at[q, role],
-            send_sem=send.at[q, 10 + role],
-            recv_sem=relay_recv.at[q, role],
-            device_id=down,
-            device_id_type=MESH,
-        )
-
-    def crossing(q, role):
-        return pltpu.make_async_remote_copy(
-            src_ref=relay.at[q, role],
-            dst_ref=panel.at[chunk(q), peer_slot(role)],
-            send_sem=send.at[q, 12 + role],
-            recv_sem=recv.at[chunk(q), peer_slot(role)],
-            device_id=y_peer,
-            device_id_type=MESH,
-        )
-
     def white_copy(q, g):
         return pltpu.make_async_remote_copy(
             src_ref=white.at[g],
             dst_ref=white.at[g],
-            send_sem=send.at[q, 14],
+            send_sem=send.at[q, 10],
             recv_sem=white_recv.at[g],
             device_id=y_peer,
             device_id_type=MESH,
@@ -299,8 +275,15 @@
 
     def choose(q, cells):
         picked = jnp.dot(pick, cells, preferred_element_type=jnp.float32)
+        mine = picked[0:16].astype(jnp.bfloat16)
+        for role in range(2):
+            @pl.when(rank == role)
+            def _():
+                panel[chunk(q), slot(role, x, c)] = mine
+                remote(q, slot(role, x, c), 1, ranked(2)).start()
+                remote(q, slot(role, x, c), 0, ranked(1 - role)).start()
+                spread(q, role)
         chan[chunk(q)] = picked[16:]
-        return picked[0:16].astype(jnp.bfloat16)
 
     def whiten(q):
         blocks = part // STEP
@@ -334,96 +317,29 @@
             axis=0,
         )
         white[g] = cells
-        mine = choose(q, cells)
-
-        @pl.when(rank == 0)
-        def _():
-            panel[g, slot(0, x, c)] = mine
-            remote(q, slot(0, x, c), 0, up).start()
-            spread(q, 0)
-
-        @pl.when(rank == 1)
-        def _():
-            panel[g, slot(1, x, c)] = mine
-            remote(q, slot(1, x, c), 0, up).start()
-            remote(q, slot(1, x, c), 1, down).start()
-            spread(q, 1)
+        white_copy(q, g).start()
+        choose(q, cells)
+
+    def along_y(q):
+        g = chunk(q)
+        white_copy(q, g).wait_recv()
+        choose(q, white[g])
+
+    def along_z(q):
+        for role in range(2):
+            @pl.when(rank == 1 - role)
+            def _():
+                arrived(q, slot(role, x, c))
+                spread(q, role)
 
         @pl.when(rank == 2)
-        def _():
-            relay[q, 1] = mine
-            relayed(q, 1).start()
-
-        @pl.when(rank == 3)
-        def _():
-            relay[q, 0] = mine
-            relayed(q, 0).start()
-
-        white_copy(q, g).start()
-
-    def along_z(q):
-        @pl.when(rank == 0)
-        def _():
-            arrived(q, slot(1, x, c))
-            spread(q, 1)
-            for role in range(2):
-                relayed(q, role).wait_recv()
-                crossing(q, role).start()
-
-        @pl.when(rank == 1)
-        def _():
-            arrived(q, slot(0, x, c))
-            remote(q, slot(0, x, c), 2, up).start()
-            spread(q, 0)
-            for role in (1, 0):
-                relayed(q, role).wait_recv()
-                relayed(q, role).start()
-                crossing(q, role).start()
-
-        @pl.when(rank == 2)
-        def _():
-            relayed(q, 0).wait_recv()
-            relayed(q, 0).start()
-            for role in (1, 0):
-                arrived(q, slot(role, x, c))
-                remote(q, slot(role, x, c), 2 + role, up).start()
-                spread(q, role)
-
-        @pl.when(rank == 3)
         def _():
             for role in (1, 0):
                 arrived(q, slot(role, x, c))
+                remote(q, slot(role, x, c), 2 + role, ranked(3)).start()
                 spread(q, role)
 
-    def along_y(q):
-        g = chunk(q)
-        white_copy(q, g).wait_recv()
-        mine = choose(q, white[g])
-
-        @pl.when(rank == 0)
-        def _():
-            panel[g, slot(0, x, c)] = mine
-            remote(q, slot(0, x, c), 0, up).start()
-            spread(q, 0)
-
-        @pl.when(rank == 1)
-        def _():
-            panel[g, slot(1, x, c)] = mine
-            remote(q, slot(1, x, c), 1, down).start()
-            spread(q, 1)
-
-    def after_y(q):
-        @pl.when(rank == 0)
-        def _():
-            arrived(q, slot(1, x, c))
-            spread(q, 1)
-
-        @pl.when(rank == 1)
-        def _():
-            arrived(q, slot(0, x, c))
-            spread(q, 0)
-
-        @pl.when(rank > 1)
+        @pl.when(rank == 3)
         def _():
             for role in (1, 0):
                 arrived(q, slot(role, x, c))
@@ -510,22 +426,22 @@
     amp[0:16, edge] = high
     amp[16:32, edge] = low
     whiten(1)
+    along_y(3)
+    along_y(2)
     along_z(0)
     table_part(0)
     along_z(1)
-    along_y(3)
     along_x(0)
     table_part(1)
-    along_y(2)
-    after_y(3)
+    along_z(3)
     along_x(1)
+    table_part(3)
     correlate(0)
-    after_y(2)
+    along_z(2)
     along_x(3)
-    table_part(3)
+    table_part(2)
     correlate(1)
     along_x(2)
-    table_part(2)
     correlate(3)
     correlate(2)
 
@@ -533,32 +449,20 @@
         remote(q, 0, kind, core_peer).wait_send()
 
     for q in range(CHUNKS):
-        own_half = q < 2
-
-        @pl.when(rank == 0)
+        @pl.when(rank < 2)
         def _():
-            for kind in (0, 12, 13) if own_half else (0,):
-                sent(q, kind)
-
-        @pl.when(rank == 1)
+            sent(q, 0)
+            sent(q, 1)
+
+        @pl.when(rank == 2)
         def _():
-            for kind in (0, 1, 2, 10, 11, 12, 13) if own_half else (1,):
-                sent(q, kind)
-
-        if own_half:
-            white_copy(q, chunk(q)).wait_send()
-
-            @pl.when(rank == 2)
-            def _():
-                for kind in (2, 3, 10, 11):
-                    sent(q, kind)
-
-            @pl.when(rank == 3)
-            def _():
-                sent(q, 10)
+            sent(q, 2)
+            sent(q, 3)
 
         for kind in range(4, 10):
             sent(q, kind)
+    for q in range(2):
+        white_copy(q, chunk(q)).wait_send()
 
 
 def fused_body(spectra, dead_mask, seg_offsets, src_index):
@@ -583,7 +487,6 @@
             pltpu.VMEM((CHUNKS, 32, part), bf16),
             pltpu.VMEM((CHUNKS, ch_count * 16, part), f32),
             pltpu.VMEM((CHUNKS, 8, 16, part), bf16),
-            pltpu.VMEM((2, 2, 16, part), bf16),
             pltpu.VMEM((2 * bins, LAGS), bf16),
             pltpu.VMEM((ch_count * shares, 2 * part), bf16),
             pltpu.VMEM((bins // STEP, LAGS), f32),
@@ -591,9 +494,8 @@
             pltpu.VMEM((STEP, LAGS), f32),
             pltpu.VMEM((STEP, LAGS), f32),
             pltpu.SemaphoreType.DMA((2,)),
-            pltpu.SemaphoreType.DMA((CHUNKS, 15)),
+            pltpu.SemaphoreType.DMA((CHUNKS, 11)),
             pltpu.SemaphoreType.DMA((CHUNKS, 8)),
-            pltpu.SemaphoreType.DMA((2, 2)),
             pltpu.SemaphoreType.DMA((CHUNKS,)),
         ],
         compiler_params=pltpu.CompilerParams(

time: 31 us -> 29.5 us (0.952)
  the two profiles are of different devices: /device:TPU:0 before, /device:TPU:5 now
where the time goes in v4:
time: 29.5 us; the launch traced here: 29 us
  Pallas kernels  26.6 us (90%)
  local copies, waits for them, and re-layouts  2.4 us (8%)
    pallas_call x1, Pallas kernels, fused_body(): pl.pallas_call(kernel, out_shape=jax.ShapeDtypeStruct((ch_count * shares,...  26.6 us
    unnamed x8, local copies, waits for them, and re-layouts  2.37 us

profile of v4, /device:TPU:5, one launch (start us, length us, event | category | flops | bytes accessed | tf_op | source)
XLA Modules:
  0.0 29.0 jit_solution(13252576278813321256)
XLA Ops:
  0.0 1.0 %copy.6 = bf16[2,2,6,2048]{3,2,1,0:T(8,128)(2,1)S(1)} copy(bf16[2,2,6,2048]{3,0,1,2:T(2,128)(2,1)} %bitcast.9) | data formatting | bytes 196608
  1.0 0.0 copy-start.2
  1.0 0.0 copy-start
  1.0 0.0 copy-start.1
  1.0 0.6 %copy-done.2 = s32[64]{0:T(128)S(1)} copy-done((s32[64]{0:T(128)S(1)}, s32[64]{0:T(128)}, u32[]{:S(2)}) %copy-start.2) | copy-done | bytes 280
  1.6 0.1 copy-done
  1.7 0.0 copy-done.1
  1.7 26.6 %shard_map.46 = f32[192,512]{1,0:T(8,128)S(1)} custom-call(bf16[32,2048]{1,0:T(8,128)(2,1)S(1)} %bitcast.7, s32[2,6]{1,0:T(2,128)S(1)} %bitcast.8, s32[6]{0:T(128)S(1)} %copy-done.1, s32[64]{0:T(128)S(1)} %copy-done.2), custom_call_target="tpu_custom_call" | custom-call | tf_op jit(solution)/shard_map/pallas_call | solution.py:479
  28.3 0.7 %copy.8 = f32[32,6,512]{2,0,1:T(8,128)} copy(f32[32,6,512]{2,0,1:T(8,128)S(1)} %bitcast.6) | data formatting | bytes 786432
  (1 shorter events, 0.0 us)
Async XLA Ops:
  1.0 0.7 %copy-start.2 = (s32[64]{0:T(128)S(1)}, s32[64]{0:T(128)}, u32[]{:S(2)}) copy-start(s32[64]{0:T(128)} %src_ref.1) | copy-start | bytes 772
  1.0 0.7 %copy-start = (s32[6,2]{0,1:T(2,128)S(1)}, s32[6,2]{0,1:T(2,128)}, u32[]{:S(2)}) copy-start(s32[6,2]{0,1:T(2,128)} %param.6) | copy-start | bytes 148
  1.0 0.7 %copy-start.1 = (s32[6]{0:T(128)S(1)}, s32[6]{0:T(128)}, u32[]{:S(2)}) copy-start(s32[6]{0:T(128)} %dead_ref.1) | copy-start | bytes 76

commit v5 on v4

--- a/solution.py
+++ b/solution.py
@@ -139,6 +139,7 @@
 
 
 CHUNKS = 4
+ORDER = (0, 1, 3, 2)
 STEP = 128
 
 
@@ -283,7 +284,7 @@
                 remote(q, slot(role, x, c), 1, ranked(2)).start()
                 remote(q, slot(role, x, c), 0, ranked(1 - role)).start()
                 spread(q, role)
-        chan[chunk(q)] = picked[16:]
+        chan[chunk(q)] = picked[16:] * (1.0 / math.sqrt(2))
 
     def whiten(q):
         blocks = part // STEP
@@ -378,13 +379,25 @@
 
         lax.fori_loop(0, part // STEP, table_step, 0)
 
-    def correlate(q):
+    def multiply(place):
+        g = chunk(ORDER[place])
+        product = jnp.dot(
+            rows[place % 2],
+            table[pl.ds(pl.multiple_of(g * 2 * part, 16), 2 * part), :],
+            preferred_element_type=jnp.float32,
+        ) * (1.0 / math.sqrt(bins))
+        if place == 0:
+            o_ref[...] = product
+        else:
+            o_ref[...] += product
+
+    def correlate(place):
+        q = ORDER[place]
         for role in range(2):
             for xv in range(2):
                 arrived(q, slot(role, xv, 1 - c))
         g = chunk(q)
         first = lax.broadcasted_iota(jnp.int32, (8, STEP), 0) < 4
-        norm = 1.0 / math.sqrt(2)
 
         def cross(a, carry):
             lanes = pl.ds(pl.multiple_of(a * STEP, STEP), STEP)
@@ -402,48 +415,42 @@
                         keep = jnp.where(first, terms[b], terms[b + 1])
                         move = jnp.where(first, terms[b + 1], terms[b])
                         pairs.append(keep + pltpu.roll(move, 4, 0))
-                    joined = jnp.concatenate(pairs, axis=0) * norm
+                    joined = jnp.concatenate(pairs, axis=0)
                     cols = pl.ds(pl.multiple_of((2 * a + imag) * STEP, STEP), STEP)
-                    rows[ch * 32 : ch * 32 + 32, cols] = joined.astype(jnp.bfloat16)
+                    rows[place % 2, ch * 32 : ch * 32 + 32, cols] = joined.astype(jnp.bfloat16)
             return carry
 
-        lax.fori_loop(0, part // STEP, cross, 0)
-        product = jnp.dot(
-            rows[...],
-            table[pl.ds(pl.multiple_of(g * 2 * part, 16), 2 * part), :],
-            preferred_element_type=jnp.float32,
-        ) * (1.0 / math.sqrt(bins))
-        if q == 0:
-            o_ref[...] = product
-        else:
-            o_ref[...] += product
+        if place > 0:
+            multiply(place - 1)
+        lax.fori_loop(0, part // STEP, cross, 0, unroll=True)
 
     whiten(0)
     table_base()
+    table_part(0)
     halo_copy.wait()
     high, low = amplitude(halo[...])
     edge = pl.ds(pl.multiple_of((1 - n) * (half + STEP), STEP), STEP)
     amp[0:16, edge] = high
     amp[16:32, edge] = low
     whiten(1)
+    table_part(1)
     along_y(3)
     along_y(2)
     along_z(0)
-    table_part(0)
     along_z(1)
     along_x(0)
-    table_part(1)
+    table_part(3)
     along_z(3)
     along_x(1)
-    table_part(3)
-    correlate(0)
     along_z(2)
     along_x(3)
+    correlate(0)
     table_part(2)
+    along_x(2)
     correlate(1)
-    along_x(2)
+    correlate(2)
     correlate(3)
-    correlate(2)
+    multiply(3)
 
     def sent(q, kind):
         remote(q, 0, kind, core_peer).wait_send()
@@ -488,7 +495,7 @@
             pltpu.VMEM((CHUNKS, ch_count * 16, part), f32),
             pltpu.VMEM((CHUNKS, 8, 16, part), bf16),
             pltpu.VMEM((2 * bins, LAGS), bf16),
-            pltpu.VMEM((ch_count * shares, 2 * part), bf16),
+            pltpu.VMEM((2, ch_count * shares, 2 * part), bf16),
             pltpu.VMEM((bins // STEP, LAGS), f32),
             pltpu.VMEM((bins // STEP, LAGS), f32),
             pltpu.VMEM((STEP, LAGS), f32),

time: 29.5 us -> 29.5 us (level)
  the two profiles are of different devices: /device:TPU:5 before, /device:TPU:6 now
where the time goes in v5:
time: 29.5 us; the launch traced here: 29.3 us
  Pallas kernels  26.9 us (91%)
  local copies, waits for them, and re-layouts  2.4 us (8%)
    pallas_call x1, Pallas kernels, fused_body(): pl.pallas_call(kernel, out_shape=jax.ShapeDtypeStruct((ch_count * shares,...  26.9 us
    unnamed x8, local copies, waits for them, and re-layouts  2.37 us

profile of v5, /device:TPU:6, one launch (start us, length us, event | category | flops | bytes accessed | tf_op | source)
XLA Modules:
  0.0 29.3 jit_solution(10199924443808463386)
XLA Ops:
  0.0 1.0 %copy.6 = bf16[2,2,6,2048]{3,2,1,0:T(8,128)(2,1)S(1)} copy(bf16[2,2,6,2048]{3,0,1,2:T(2,128)(2,1)} %bitcast.9) | data formatting | bytes 196608
  1.0 0.0 copy-start.2
  1.0 0.0 copy-start
  1.0 0.0 copy-start.1
  1.0 0.6 %copy-done.2 = s32[64]{0:T(128)S(1)} copy-done((s32[64]{0:T(128)S(1)}, s32[64]{0:T(128)}, u32[]{:S(2)}) %copy-start.2) | copy-done | bytes 280
  1.6 0.1 copy-done
  1.7 0.0 copy-done.1
  1.7 26.9 %shard_map.46 = f32[192,512]{1,0:T(8,128)S(1)} custom-call(bf16[32,2048]{1,0:T(8,128)(2,1)S(1)} %bitcast.7, s32[2,6]{1,0:T(2,128)S(1)} %bitcast.8, s32[6]{0:T(128)S(1)} %copy-done.1, s32[64]{0:T(128)S(1)} %copy-done.2), custom_call_target="tpu_custom_call" | custom-call | tf_op jit(solution)/shard_map/pallas_call | solution.py:486
  28.6 0.7 %copy.8 = f32[32,6,512]{2,0,1:T(8,128)} copy(f32[32,6,512]{2,0,1:T(8,128)S(1)} %bitcast.6) | data formatting | bytes 786432
  (1 shorter events, 0.0 us)
Async XLA Ops:
  1.0 0.7 %copy-start.2 = (s32[64]{0:T(128)S(1)}, s32[64]{0:T(128)}, u32[]{:S(2)}) copy-start(s32[64]{0:T(128)} %src_ref.1) | copy-start | bytes 772
  1.0 0.7 %copy-start = (s32[6,2]{0,1:T(2,128)S(1)}, s32[6,2]{0,1:T(2,128)}, u32[]{:S(2)}) copy-start(s32[6,2]{0,1:T(2,128)} %param.6) | copy-start | bytes 148
  1.0 0.7 %copy-start.1 = (s32[6]{0:T(128)S(1)}, s32[6]{0:T(128)}, u32[]{:S(2)}) copy-start(s32[6]{0:T(128)} %dead_ref.1) | copy-start | bytes 76

commit v6 on v5

--- a/solution.py
+++ b/solution.py
@@ -438,11 +438,11 @@
     along_y(2)
     along_z(0)
     along_z(1)
+    along_z(3)
+    along_z(2)
     along_x(0)
     table_part(3)
-    along_z(3)
     along_x(1)
-    along_z(2)
     along_x(3)
     correlate(0)
     table_part(2)

time: 29.5 us -> 27.2 us (0.922)
  the two profiles are of different devices: /device:TPU:6 before, /device:TPU:5 now
where the time goes in v6:
time: 27.2 us; the launch traced here: 27 us
  Pallas kernels  24.6 us (90%)
  local copies, waits for them, and re-layouts  2.4 us (9%)
    pallas_call x1, Pallas kernels, fused_body(): pl.pallas_call(kernel, out_shape=jax.ShapeDtypeStruct((ch_count * shares,...  24.6 us
    unnamed x8, local copies, waits for them, and re-layouts  2.37 us

profile of v6, /device:TPU:5, one launch (start us, length us, event | category | flops | bytes accessed | tf_op | source)
XLA Modules:
  0.0 27.0 jit_solution(10434589928631453324)
XLA Ops:
  0.0 1.0 %copy.6 = bf16[2,2,6,2048]{3,2,1,0:T(8,128)(2,1)S(1)} copy(bf16[2,2,6,2048]{3,0,1,2:T(2,128)(2,1)} %bitcast.9) | data formatting | bytes 196608
  1.0 0.0 copy-start.2
  1.0 0.0 copy-start
  1.0 0.0 copy-start.1
  1.0 0.6 %copy-done.2 = s32[64]{0:T(128)S(1)} copy-done((s32[64]{0:T(128)S(1)}, s32[64]{0:T(128)}, u32[]{:S(2)}) %copy-start.2) | copy-done | bytes 280
  1.6 0.1 copy-done
  1.7 0.0 copy-done.1
  1.7 24.6 %shard_map.46 = f32[192,512]{1,0:T(8,128)S(1)} custom-call(bf16[32,2048]{1,0:T(8,128)(2,1)S(1)} %bitcast.7, s32[2,6]{1,0:T(2,128)S(1)} %bitcast.8, s32[6]{0:T(128)S(1)} %copy-done.1, s32[64]{0:T(128)S(1)} %copy-done.2), custom_call_target="tpu_custom_call" | custom-call | tf_op jit(solution)/shard_map/pallas_call | solution.py:486
  26.3 0.7 %copy.8 = f32[32,6,512]{2,0,1:T(8,128)} copy(f32[32,6,512]{2,0,1:T(8,128)S(1)} %bitcast.6) | data formatting | bytes 786432
  (1 shorter events, 0.0 us)
Async XLA Ops:
  1.0 0.7 %copy-start.2 = (s32[64]{0:T(128)S(1)}, s32[64]{0:T(128)}, u32[]{:S(2)}) copy-start(s32[64]{0:T(128)} %src_ref.1) | copy-start | bytes 772
  1.0 0.7 %copy-start = (s32[6,2]{0,1:T(2,128)S(1)}, s32[6,2]{0,1:T(2,128)}, u32[]{:S(2)}) copy-start(s32[6,2]{0,1:T(2,128)} %param.6) | copy-start | bytes 148
  1.0 0.7 %copy-start.1 = (s32[6]{0:T(128)S(1)}, s32[6]{0:T(128)}, u32[]{:S(2)}) copy-start(s32[6]{0:T(128)} %dead_ref.1) | copy-start | bytes 76
